TPU v7x, 32 devices: a whole 2x2x4 slice. The times are simulated.
32 devices in a mesh: groups: 2 (over x), chan: 16 (over z, y, core).
Axes of the slice: x: 2, y: 2, z: 4, core: 2. Of those that a mesh axis runs over, the one named last changes fastest.
Arguments:
- raw: bfloat16 [5120, 4096], P('chan', 'groups'), parts along dimension 1, may hold values from -50 to 50
- taps: bfloat16 [255], replicated, may hold values from -0.375 to 0.375
- tile_dist: int32 [16, 8], P('chan', 'groups'), parts along dimension 1, may hold values from 1 to 4, as said below
- tile_count: int32 [32], P(('groups', 'chan')), parts along dimension 0, may hold values from 0 to 4
- owner: int32 [8], P('groups'), parts along dimension 0, may hold values from 0 to 15, as said below
Outputs:
- band_stack: float32 [16, 256, 128], P('chan', 'groups'), parts along dimension 1
There are 2 independent parts, one for each index of `groups`. A program takes and returns all parts, laid end to end along the dimension named above; an argument that names none is the same for every part. Nothing has to cross between parts.
Inputs may be any that keep to these rules, and one draw needn't show every extreme that they name: Each row of tile_dist holds every distance of 1 to 4 once; in row i the first tile_count[i] entries d satisfy i + d < 16. `owner`: the owners are distinct, and some band is owned by index 15.
All inputs are finite; a program needn't handle non-finite values.
Results may differ from a plain program's by a relative error of at most 0.014.
Values may be sent and summed in bfloat16 or wider, within the bound.
A program may use at most 128 MiB of HBM per device.

v0:
```python
import math
import jax
import jax.numpy as jnp
from jax import lax
from jax.sharding import PartitionSpec as P


def extended(x, sides, width):
    for axis, dim in sides:
        size, length = (lax.axis_size(axis), x.shape[dim])
        up = [(i, (i + 1) % size) for i in range(size - 1)]
        down = [(j, i) for i, j in up]
        last = lax.slice_in_dim(x, length - width, length, axis=dim)
        initial = lax.slice_in_dim(x, 0, width, axis=dim)
        before = lax.ppermute(last, axis, up)
        after = lax.ppermute(initial, axis, down)
        x = jnp.concatenate([before, x, after], axis=dim)
    return x


def passed_along(x, axis, by):
    size = lax.axis_size(axis)
    pairs = [(i, i + by) for i in range(size) if 0 <= i + by < size]
    return lax.ppermute(x, axis, pairs)


def band_matrix(taps, out_rows, in_cols):
    width = taps.shape[0]
    offset = (
        jnp.arange(in_cols, dtype=jnp.int32)[None, :]
        - 5 * jnp.arange(out_rows, dtype=jnp.int32)[:, None]
    )
    inside = (offset >= 0) & (offset < width)
    picked = jnp.take(taps, jnp.clip(offset, 0, width - 1))
    return jnp.where(inside, picked, jnp.zeros_like(picked))


def whiten(block):
    length, channels = block.shape
    bins = length // 16
    freqs = jnp.arange(1, bins + 1, dtype=jnp.int32)[:, None]
    times = jnp.arange(length, dtype=jnp.int32)[None, :]
    angle = (freqs * times % length).astype(jnp.float32) * (2.0 * math.pi / length)
    table = jnp.concatenate([jnp.cos(angle), -jnp.sin(angle)], axis=0)
    table_high = table.astype(jnp.bfloat16)
    table_low = (table - table_high.astype(jnp.float32)).astype(jnp.bfloat16)
    spectrum = jnp.dot(table_high, block, preferred_element_type=jnp.float32)
    spectrum = spectrum + jnp.dot(table_low, block, preferred_element_type=jnp.float32)
    squares = spectrum * spectrum
    power = jnp.sum(squares[:bins] + squares[bins:], axis=1) / (2 * channels)
    gain = lax.rsqrt(power + 1e-06)
    return (spectrum * jnp.concatenate([gain, gain])[:, None]).astype(jnp.bfloat16)


def cross_tile(mine, partner, scale):
    product = lax.dot_general(
        mine, partner, (((0,), (0,)), ((), ())), preferred_element_type=jnp.float32
    )
    return product * scale


def shards(raw, taps, tile_dist, tile_count, owner):
    rows = raw.shape[0]
    width = taps.shape[0]
    half = (width - 1) // 2
    out_rows = rows // 5
    banded = band_matrix(taps, out_rows, rows + 2 * half)
    padded = extended(raw, (("chan", 0),), half)
    filtered = jnp.dot(banded, padded, preferred_element_type=jnp.float32)
    decimated = filtered.astype(jnp.bfloat16)
    regrouped = lax.all_to_all(decimated, "chan", split_axis=1, concat_axis=0, tiled=True)
    whitened = whiten(regrouped)
    channels = whitened.shape[1]
    scale = 1.0 / whitened.shape[0]
    bands = tile_dist.shape[1]
    slots = jnp.arange(bands, dtype=jnp.int32) < tile_count[0]
    partner = whitened
    stacks = []
    for distance in range(1, bands + 1):
        partner = passed_along(whitened, "chan", -distance)
        listed = jnp.sum(((tile_dist[0] == distance) & slots).astype(jnp.int32))
        tile = lax.cond(
            listed > 0,
            lambda first, second: cross_tile(first, second, scale),
            lambda first, second: jnp.zeros((channels, channels), jnp.float32),
            whitened,
            partner,
        )
        stacks.append(tile)
    stacked = jnp.stack(stacks)
    totals = lax.psum(stacked, "chan")
    selected = (owner == lax.axis_index("chan")).astype(jnp.float32)
    return jnp.einsum("b,bxy->xy", selected, totals, precision=lax.Precision.HIGHEST)[None]


def solution(mesh):
    in_specs = (P("chan", "groups"), P(), P("chan", "groups"), P(("groups", "chan")), P("groups"))
    out_specs = P("chan", "groups", None)
    return jax.shard_map(shards, mesh=mesh, in_specs=in_specs, out_specs=out_specs, check_vma=False)
```

profile of v0, /device:TPU:1, one launch (start us, length us, event | category | flops | bytes accessed | tf_op | source)
XLA Modules:
  0.0 350.2 jit_solution(16321516343890510298)
XLA Ops:
  6.5 0.0 copy-start
  6.5 1.3 fusion.63
  7.9 4.5 %collective-permute-start = (bf16[127,2048]{1,0:T(8,128)(2,1)S(1)}, bf16[127,2048]{1,0:T(8,128)(2,1)S(1)}, u32[]{:S(2)}, u32[]{:S(2)}) collective-permute-start(bf16[127,2048]{1,0:T(8,128)(2,1)S(1)} %get-tuple-element.49), channel_id=1, source_target_pairs={{0,1},{1,2},{2,3},{3,4},{4,5},{5,6},{6,7},{7,8},{8,9},{9,10},{10,1... | collective-permute-start | bytes 1560584 | tf_op jit(solution)/shard_map/ppermute | solution.py:15
  12.4 1.9 collective-permute-start.1
  14.4 0.1 compare_select_fusion
  14.5 0.2 reshape.83
  14.7 0.0 copy-done
  14.7 0.0 copy-start.1
  14.7 202.9 %gather_fusion = bf16[36736]{0:T(1024)(128)(2,1)S(1)} fusion(bf16[255]{0:T(256)(128)(2,1)S(1)} %copy-done, s32[36864]{0:T(1024)S(1)} %pad_clamp_fusion), kind=kCustom, calls=%fused_computation | custom fusion | bytes 293888 | tf_op jit(solution)/shard_map/jit(_take)/gather | solution.py:34
  217.7 0.2 reshape.82
  217.9 0.0 collective-permute-done
  217.9 0.0 collective-permute-done.1
  217.9 0.0 copy-done.1
  217.9 1.9 fusion.13
  219.8 0.8 copy.13
  220.6 6.5 %all-to-all-start = ((bf16[64,16,128]{2,0,1:T(8,128)(2,1)}), bf16[64,16,128]{2,0,1:T(8,128)(2,1)S(1)}, u32[]{:S(2)}, u32[]{:S(2)}) async-start(bf16[64,16,128]{2,0,1:T(8,128)(2,1)} %bitcast.58), calls=%async_computation | async-start | bytes 524288 | tf_op jit(solution)/shard_map/all_to_all | solution.py:71
  227.0 0.0 copy-start.3
  227.1 0.0 all-reduce.2.cloned.1.call-start
  227.8 1.1 fusion.35
  228.9 7.7 %all-to-all-done = bf16[64,16,128]{2,0,1:T(8,128)(2,1)S(1)} async-done(((bf16[64,16,128]{2,0,1:T(8,128)(2,1)}), bf16[64,16,128]{2,0,1:T(8,128)(2,1)S(1)}, u32[]{:S(2)}, u32[]{:S(2)}) %all-to-all-start) | async-done | bytes 262176 | tf_op jit(solution)/shard_map/all_to_all | solution.py:71
  236.5 0.2 fusion.17
  236.8 0.0 copy-start.2
  236.8 0.2 fusion.64
  237.0 0.1 fusion.43
  237.1 0.1 pad_maximum_fusion.2
  237.2 0.1 multiply_convert_fusion
  237.3 2.6 collective-permute-start.2
  239.9 1.3 collective-permute-start.3
  241.2 1.3 collective-permute-start.4
  242.5 1.3 collective-permute-start.5
  243.8 0.0 copy-done.3
  243.8 0.7 fusion.50
  247.0 0.0 collective-permute-done.2
  247.1 0.0 collective-permute-done.3
  247.1 0.2 conditional.5
  247.1 0.2 fusion.1
  247.3 0.5 collective-permute-done.4
  247.8 1.3 collective-permute-done.5
  249.2 0.2 conditional.7
  249.2 0.2 fusion.3
  249.4 0.7 pad_maximum_fusion.1
  250.1 0.0 all-reduce.2.cloned.1.call-update
  250.1 91.1 %all-reduce.2.cloned.1.call-done = f32[4,128,128]{2,1,0:T(8,128)} async-done(((f32[4,128,128]{2,1,0:T(8,128)}), f32[4,128,128]{2,1,0:T(8,128)}) %all-reduce.2.cloned.1.call-update) | async-done | bytes 262160 | tf_op jit(solution)/shard_map/psum | solution.py:91
  341.3 0.0 copy-done.2
  341.3 2.1 fusion.22
  (8 shorter events, 0.1 us)
Async XLA Ops:
  6.5 8.2 %copy-start = (bf16[255]{0:T(256)(128)(2,1)S(1)}, bf16[255]{0:T(256)(128)(2,1)}, u32[]{:S(2)}) copy-start(bf16[255]{0:T(256)(128)(2,1)} %param.14) | copy-start | bytes 1534
  7.9 210.0 %collective-permute-start = (bf16[127,2048]{1,0:T(8,128)(2,1)S(1)}, bf16[127,2048]{1,0:T(8,128)(2,1)S(1)}, u32[]{:S(2)}, u32[]{:S(2)}) collective-permute-start(bf16[127,2048]{1,0:T(8,128)(2,1)S(1)} %get-tuple-element.49), channel_id=1, source_target_pairs={{0,1},{1,2},{2,3},{3,4},{4,5},{5,6},{6,7},{7,8},{8,9},{9,10},{10,1... | collective-permute-start | bytes 1560584 | tf_op jit(solution)/shard_map/ppermute | solution.py:15
  12.4 205.5 %collective-permute-start.1 = (bf16[127,2048]{1,0:T(8,128)(2,1)S(1)}, bf16[127,2048]{1,0:T(8,128)(2,1)}, u32[]{:S(2)}, u32[]{:S(2)}) collective-permute-start(bf16[127,2048]{1,0:T(8,128)(2,1)S(1)} %get-tuple-element.50), channel_id=1, source_target_pairs={{1,0},{2,1},{3,2},{4,3},{5,4},{6,5},{7,6},{8,7},{9,8},{10,9},{11,1... | collective-permute-start | bytes 1560584 | tf_op jit(solution)/shard_map/ppermute | solution.py:16
  14.7 203.2 %copy-start.1 = (bf16[320,2048]{1,0:T(8,128)(2,1)S(1)}, bf16[320,2048]{1,0:T(8,128)(2,1)}, u32[]{:S(2)}) copy-start(bf16[320,2048]{1,0:T(8,128)(2,1)} %param.13) | copy-start | bytes 3932164
  220.6 15.9 %all-to-all-start = ((bf16[64,16,128]{2,0,1:T(8,128)(2,1)}), bf16[64,16,128]{2,0,1:T(8,128)(2,1)S(1)}, u32[]{:S(2)}, u32[]{:S(2)}) async-start(bf16[64,16,128]{2,0,1:T(8,128)(2,1)} %bitcast.58), calls=%async_computation | async-start | bytes 524288 | tf_op jit(solution)/shard_map/all_to_all | solution.py:71
  227.0 16.7 %copy-start.3 = (s32[1,4]{1,0:T(1,128)S(1)}, s32[1,4]{1,0:T(1,128)}, u32[]{:S(2)}) copy-start(s32[1,4]{1,0:T(1,128)} %param.15) | copy-start | bytes 52
  227.1 114.2 %all-reduce.2.cloned.1.call-start = ((), (), s32[]{:S(2)}) async-start(), calls=%async_computation.1 | async-start | bytes 524288 | tf_op jit(solution)/shard_map/psum | solution.py:91
  236.8 104.5 %copy-start.2 = (s32[4]{0:T(128)S(1)}, s32[4]{0:T(128)}, u32[]{:S(2)}) copy-start(s32[4]{0:T(128)} %param.17) | copy-start | bytes 52
  237.3 9.7 %collective-permute-start.2 = (bf16[128,128]{1,0:T(8,128)(2,1)S(1)}, bf16[128,128]{1,0:T(8,128)(2,1)S(1)}, u32[]{:S(2)}, u32[]{:S(2)}) collective-permute-start(bf16[128,128]{1,0:T(8,128)(2,1)S(1)} %multiply_convert_fusion), channel_id=1, source_target_pairs={{1,0},{2,1},{3,2},{4,3},{5,4},{6,5},{7,6},{8,7},{9,8},{10,9},{11,1... | collective-permute-start | bytes 98312 | tf_op jit(solution)/shard_map/ppermute | solution.py:24
  239.9 7.2 %collective-permute-start.3 = (bf16[128,128]{1,0:T(8,128)(2,1)S(1)}, bf16[128,128]{1,0:T(8,128)(2,1)S(1)}, u32[]{:S(2)}, u32[]{:S(2)}) collective-permute-start(bf16[128,128]{1,0:T(8,128)(2,1)S(1)} %multiply_convert_fusion), channel_id=1, source_target_pairs={{2,0},{3,1},{4,2},{5,3},{6,4},{7,5},{8,6},{9,7},{10,8},{11,9},{12,... | collective-permute-start | bytes 98312 | tf_op jit(solution)/shard_map/ppermute | solution.py:24
  241.2 6.7 %collective-permute-start.4 = (bf16[128,128]{1,0:T(8,128)(2,1)S(1)}, bf16[128,128]{1,0:T(8,128)(2,1)S(1)}, u32[]{:S(2)}, u32[]{:S(2)}) collective-permute-start(bf16[128,128]{1,0:T(8,128)(2,1)S(1)} %multiply_convert_fusion), channel_id=1, source_target_pairs={{3,0},{4,1},{5,2},{6,3},{7,4},{8,5},{9,6},{10,7},{11,8},{12,9},{13... | collective-permute-start | bytes 98312 | tf_op jit(solution)/shard_map/ppermute | solution.py:24
  242.5 6.7 %collective-permute-start.5 = (bf16[128,128]{1,0:T(8,128)(2,1)S(1)}, bf16[128,128]{1,0:T(8,128)(2,1)S(1)}, u32[]{:S(2)}, u32[]{:S(2)}) collective-permute-start(bf16[128,128]{1,0:T(8,128)(2,1)S(1)} %multiply_convert_fusion), channel_id=1, source_target_pairs={{4,0},{5,1},{6,2},{7,3},{8,4},{9,5},{10,6},{11,7},{12,8},{13,9},{1... | collective-permute-start | bytes 98312 | tf_op jit(solution)/shard_map/ppermute | solution.py:24
Sparse Core Ops, SparseCore 0:
  250.2 90.9 all-reduce.1
where the time goes:
time: 351 us; the launch traced here: 350 us
  local copies, waits for them, and re-layouts  205 us (58%)
  waiting for transfers between devices  101 us (29%)
  starting transfers between devices  19.4 us (6%)
  between operations  16.8 us (5%)
  matrix products  4.78 us (1%)
    gather x2, local copies, waits for them, and re-layouts, band_matrix(): picked = jnp.take(taps, jnp.clip(offset, 0, width - 1))  203 us
    psum x1, waiting for transfers between devices, shards(): totals = lax.psum(stacked, 'chan')  91.1 us
    all_to_all x1, waiting for transfers between devices, shards(): lax.all_to_all(decimated, 'chan', split_axis=1, concat_axis=0, tiled=True)  7.67 us
  transfers between devices with their start and end apart: 8, of which 4 were waited for; matrix products, arithmetic and copies ran while one was open for 59% of the time, Pallas kernels for 0%

commit v1 on v0

--- a/solution.py
+++ b/solution.py
@@ -3,6 +3,18 @@
 import jax.numpy as jnp
 from jax import lax
 from jax.sharding import PartitionSpec as P
+
+
+def in_blocks(value, dim, length):
+    shape = value.shape
+    tiles = value.reshape(*shape[:dim], length, shape[dim] // length, *shape[dim + 1 :])
+    return jnp.moveaxis(tiles, dim, 0)
+
+
+def in_order(blocks, dim):
+    shape = list(blocks.shape[1:])
+    shape[dim] *= blocks.shape[0]
+    return jnp.moveaxis(blocks, 0, dim).reshape(shape)
 
 
 def extended(x, sides, width):
@@ -68,7 +80,14 @@
     padded = extended(raw, (("chan", 0),), half)
     filtered = jnp.dot(banded, padded, preferred_element_type=jnp.float32)
     decimated = filtered.astype(jnp.bfloat16)
-    regrouped = lax.all_to_all(decimated, "chan", split_axis=1, concat_axis=0, tiled=True)
+    count, here = (lax.axis_size("chan"), lax.axis_index("chan"))
+    tiles = in_blocks(decimated, 1, count)
+    gathered = [tiles[here]]
+    for step in range(1, count):
+        sent = tiles[here ^ step]
+        gathered.append(lax.ppermute(sent, "chan", [(i_2, i_2 ^ step) for i_2 in range(count)]))
+    tiles = jnp.stack(gathered)[here ^ jnp.arange(count)]
+    regrouped = in_order(tiles, 0)
     whitened = whiten(regrouped)
     channels = whitened.shape[1]
     scale = 1.0 / whitened.shape[0]

time: 351 us -> 364 us (1.037)
  starting transfers between devices: 19.4 us -> 34.3 us
    ppermute x0 -> x15, starting transfers between devices: none -> 21.6 us  [shards(): lax.ppermute(sent, 'chan', [(i_2, i_2 ^ step) for i_2 in range(count)])]
    all_to_all x1 -> x0, waiting for transfers between devices: 7.67 us -> none  [shards(): lax.all_to_all(decimated, 'chan', split_axis=1, concat_axis=0, tiled=True)]
    all_to_all x1 -> x0, starting transfers between devices: 6.45 us -> none  [shards(): lax.all_to_all(decimated, 'chan', split_axis=1, concat_axis=0, tiled=True)]
    ppermute x0 -> x15, waiting for transfers between devices: none -> 4.6 us  [shards(): lax.ppermute(sent, 'chan', [(i_2, i_2 ^ step) for i_2 in range(count)])]
  transfers between devices with their start and end apart: 8 -> 22, of which waited for: 4 -> 4; matrix products, arithmetic and copies ran while one was open for 59% -> 57% of each run, Pallas kernels for 0% -> 0%
where the time goes in v1:
time: 364 us
  local copies, waits for them, and re-layouts  206 us (57%)
  waiting for transfers between devices  98.2 us (27%)
  starting transfers between devices  34.3 us (9%)
  between operations  17.1 us (5%)
  matrix products  4.78 us (1%)
    gather x2, local copies, waits for them, and re-layouts, band_matrix(): picked = jnp.take(taps, jnp.clip(offset, 0, width - 1))  203 us
    psum x1, waiting for transfers between devices, shards(): totals = lax.psum(stacked, 'chan')  93.5 us
    ppermute x15, starting transfers between devices, shards(): lax.ppermute(sent, 'chan', [(i_2, i_2 ^ step) for i_2 in range(count)])  21.6 us
  transfers between devices with their start and end apart: 22, of which 4 were waited for; matrix products, arithmetic and copies ran while one was open for 57% of the time, Pallas kernels for 0%

profile of v1, /device:TPU:1, one launch (start us, length us, event | category | flops | bytes accessed | tf_op | source)
XLA Modules:
  0.0 363.8 jit_solution(743818498014967686)
XLA Ops:
  6.5 1.3 fusion.64
  7.9 2.0 collective-permute-start.1
  9.9 4.5 %collective-permute-start = (bf16[127,2048]{1,0:T(8,128)(2,1)S(1)}, bf16[127,2048]{1,0:T(8,128)(2,1)}, u32[]{:S(2)}, u32[]{:S(2)}) collective-permute-start(bf16[127,2048]{1,0:T(8,128)(2,1)S(1)} %get-tuple-element.49), channel_id=1, source_target_pairs={{0,1},{1,2},{2,3},{3,4},{4,5},{5,6},{6,7},{7,8},{8,9},{9,10},{10,1... | collective-permute-start | bytes 1560584 | tf_op jit(solution)/shard_map/ppermute | solution.py:27
  15.1 0.1 compare_select_fusion
  15.2 0.2 reshape.135
  15.4 0.0 copy-start.1
  15.5 202.9 %gather_fusion = bf16[36736]{0:T(1024)(128)(2,1)S(1)} fusion(bf16[255]{0:T(256)(128)(2,1)S(1)} %copy-done, s32[36864]{0:T(1024)S(1)} %pad_clamp_fusion), kind=kCustom, calls=%fused_computation | custom fusion | bytes 293888 | tf_op jit(solution)/shard_map/jit(_take)/gather | solution.py:46
  218.4 0.2 reshape.134
  218.7 1.1 fusion.35
  219.8 0.0 collective-permute-done.1
  219.8 0.0 collective-permute-done
  219.9 1.9 fusion.13
  221.8 0.8 constant_dynamic-slice_fusion
  222.6 0.1 collective-permute-start.2
  222.7 2.1 collective-permute-start.3
  224.9 0.5 collective-permute-start.4
  225.3 1.3 collective-permute-start.5
  226.6 0.7 collective-permute-start.6
  227.5 0.0 collective-permute-done.2
  227.5 2.1 collective-permute-start.7
  229.6 0.0 collective-permute-done.3
  229.6 0.5 collective-permute-start.8
  230.1 0.0 collective-permute-done.4
  230.1 2.2 collective-permute-start.9
  232.3 0.0 collective-permute-done.5
  232.3 0.7 collective-permute-start.10
  233.0 0.0 collective-permute-done.6
  233.0 2.9 collective-permute-start.11
  236.0 0.6 collective-permute-start.12
  236.5 0.0 collective-permute-done.8
  236.5 2.6 collective-permute-start.13
  239.1 1.2 collective-permute-start.14
  240.3 0.0 collective-permute-done.10
  240.3 2.6 collective-permute-start.15
  242.9 0.0 collective-permute-done.11
  242.9 1.6 collective-permute-start.16
  244.6 0.0 collective-permute-done.12
  244.6 0.0 collective-permute-done.13
  244.6 0.0 copy-start.3
  244.6 1.1 collective-permute-done.15
  245.7 3.5 collective-permute-done.16
  249.2 0.6 gather_fusion.1
  249.8 0.2 fusion.25
  250.0 0.0 copy-start.2
  250.0 0.2 fusion.65
  250.3 0.1 fusion.43
  250.4 0.1 pad_maximum_fusion.2
  250.5 0.1 multiply_convert_fusion
  250.6 1.3 collective-permute-start.20
  251.9 1.3 collective-permute-start.19
  253.2 1.3 collective-permute-start.18
  254.5 2.4 collective-permute-start.17
  256.8 0.8 fusion.51
  260.1 0.0 collective-permute-done.20
  260.1 0.2 conditional.7
  260.1 0.2 fusion.3
  260.4 0.0 collective-permute-done.18
  260.4 0.2 conditional.5
  260.4 0.2 fusion.1
  260.6 0.1 collective-permute-done.17
  260.7 0.7 pad_maximum_fusion.1
  261.4 0.0 all-reduce.2.cloned.1.call-update
  261.4 93.5 %all-reduce.2.cloned.1.call-done = f32[4,128,128]{2,1,0:T(8,128)} async-done(((f32[4,128,128]{2,1,0:T(8,128)}), f32[4,128,128]{2,1,0:T(8,128)}) %all-reduce.2.cloned.1.call-update) | async-done | bytes 262160 | tf_op jit(solution)/shard_map/psum | solution.py:110
  354.9 2.1 fusion.21
  (52 shorter events, 0.4 us)
Async XLA Ops:
  6.5 8.9 %copy-start = (bf16[255]{0:T(256)(128)(2,1)S(1)}, bf16[255]{0:T(256)(128)(2,1)}, u32[]{:S(2)}) copy-start(bf16[255]{0:T(256)(128)(2,1)} %param.14) | copy-start | bytes 1534
  6.5 348.3 %all-reduce.2.cloned.1.call-start = ((), (), s32[]{:S(2)}) async-start(), calls=%async_computation | async-start | bytes 524288 | tf_op jit(solution)/shard_map/psum | solution.py:110
  7.9 211.9 %collective-permute-start.1 = (bf16[127,2048]{1,0:T(8,128)(2,1)S(1)}, bf16[127,2048]{1,0:T(8,128)(2,1)S(1)}, u32[]{:S(2)}, u32[]{:S(2)}) collective-permute-start(bf16[127,2048]{1,0:T(8,128)(2,1)S(1)} %get-tuple-element.50), channel_id=1, source_target_pairs={{1,0},{2,1},{3,2},{4,3},{5,4},{6,5},{7,6},{8,7},{9,8},{10,9},{11,1... | collective-permute-start | bytes 1560584 | tf_op jit(solution)/shard_map/ppermute | solution.py:28
  9.9 210.0 %collective-permute-start = (bf16[127,2048]{1,0:T(8,128)(2,1)S(1)}, bf16[127,2048]{1,0:T(8,128)(2,1)}, u32[]{:S(2)}, u32[]{:S(2)}) collective-permute-start(bf16[127,2048]{1,0:T(8,128)(2,1)S(1)} %get-tuple-element.49), channel_id=1, source_target_pairs={{0,1},{1,2},{2,3},{3,4},{4,5},{5,6},{6,7},{7,8},{8,9},{9,10},{10,1... | collective-permute-start | bytes 1560584 | tf_op jit(solution)/shard_map/ppermute | solution.py:27
  15.4 204.4 %copy-start.1 = (bf16[320,2048]{1,0:T(8,128)(2,1)S(1)}, bf16[320,2048]{1,0:T(8,128)(2,1)}, u32[]{:S(2)}) copy-start(bf16[320,2048]{1,0:T(8,128)(2,1)} %param.13) | copy-start | bytes 3932164
  222.6 4.9 %collective-permute-start.2 = (bf16[64,128]{1,0:T(8,128)(2,1)S(1)}, bf16[64,128]{1,0:T(8,128)(2,1)S(1)}, u32[]{:S(2)}, u32[]{:S(2)}) collective-permute-start(bf16[64,128]{1,0:T(8,128)(2,1)S(1)} %bitcast.154), channel_id=1, source_target_pairs={{0,1},{1,0},{2,3},{3,2},{4,5},{5,4},{6,7},{7,6},{8,9},{9,8},{10,11... | collective-permute-start | bytes 49160 | tf_op jit(solution)/shard_map/ppermute | solution.py:88
  222.7 6.9 %collective-permute-start.3 = (bf16[64,128]{1,0:T(8,128)(2,1)S(1)}, bf16[64,128]{1,0:T(8,128)(2,1)S(1)}, u32[]{:S(2)}, u32[]{:S(2)}) collective-permute-start(bf16[64,128]{1,0:T(8,128)(2,1)S(1)} %bitcast.153), channel_id=1, source_target_pairs={{0,2},{1,3},{2,0},{3,1},{4,6},{5,7},{6,4},{7,5},{8,10},{9,11},{10,... | collective-permute-start | bytes 49160 | tf_op jit(solution)/shard_map/ppermute | solution.py:88
  224.9 5.2 %collective-permute-start.4 = (bf16[64,128]{1,0:T(8,128)(2,1)S(1)}, bf16[64,128]{1,0:T(8,128)(2,1)S(1)}, u32[]{:S(2)}, u32[]{:S(2)}) collective-permute-start(bf16[64,128]{1,0:T(8,128)(2,1)S(1)} %bitcast.152), channel_id=1, source_target_pairs={{0,3},{1,2},{2,1},{3,0},{4,7},{5,6},{6,5},{7,4},{8,11},{9,10},{10,... | collective-permute-start | bytes 49160 | tf_op jit(solution)/shard_map/ppermute | solution.py:88
  225.3 7.0 %collective-permute-start.5 = (bf16[64,128]{1,0:T(8,128)(2,1)S(1)}, bf16[64,128]{1,0:T(8,128)(2,1)S(1)}, u32[]{:S(2)}, u32[]{:S(2)}) collective-permute-start(bf16[64,128]{1,0:T(8,128)(2,1)S(1)} %bitcast.151), channel_id=1, source_target_pairs={{0,4},{1,5},{2,6},{3,7},{4,0},{5,1},{6,2},{7,3},{8,12},{9,13},{10,... | collective-permute-start | bytes 49160 | tf_op jit(solution)/shard_map/ppermute | solution.py:88
  226.6 6.4 %collective-permute-start.6 = (bf16[64,128]{1,0:T(8,128)(2,1)S(1)}, bf16[64,128]{1,0:T(8,128)(2,1)S(1)}, u32[]{:S(2)}, u32[]{:S(2)}) collective-permute-start(bf16[64,128]{1,0:T(8,128)(2,1)S(1)} %bitcast.150), channel_id=1, source_target_pairs={{0,5},{1,4},{2,7},{3,6},{4,1},{5,0},{6,3},{7,2},{8,13},{9,12},{10,... | collective-permute-start | bytes 49160 | tf_op jit(solution)/shard_map/ppermute | solution.py:88
  227.5 8.5 %collective-permute-start.7 = (bf16[64,128]{1,0:T(8,128)(2,1)S(1)}, bf16[64,128]{1,0:T(8,128)(2,1)S(1)}, u32[]{:S(2)}, u32[]{:S(2)}) collective-permute-start(bf16[64,128]{1,0:T(8,128)(2,1)S(1)} %bitcast.149), channel_id=1, source_target_pairs={{0,6},{1,7},{2,4},{3,5},{4,2},{5,3},{6,0},{7,1},{8,14},{9,15},{10,... | collective-permute-start | bytes 49160 | tf_op jit(solution)/shard_map/ppermute | solution.py:88
  229.6 6.9 %collective-permute-start.8 = (bf16[64,128]{1,0:T(8,128)(2,1)S(1)}, bf16[64,128]{1,0:T(8,128)(2,1)S(1)}, u32[]{:S(2)}, u32[]{:S(2)}) collective-permute-start(bf16[64,128]{1,0:T(8,128)(2,1)S(1)} %bitcast.148), channel_id=1, source_target_pairs={{0,7},{1,6},{2,5},{3,4},{4,3},{5,2},{6,1},{7,0},{8,15},{9,14},{10,... | collective-permute-start | bytes 49160 | tf_op jit(solution)/shard_map/ppermute | solution.py:88
  230.1 9.0 %collective-permute-start.9 = (bf16[64,128]{1,0:T(8,128)(2,1)S(1)}, bf16[64,128]{1,0:T(8,128)(2,1)S(1)}, u32[]{:S(2)}, u32[]{:S(2)}) collective-permute-start(bf16[64,128]{1,0:T(8,128)(2,1)S(1)} %bitcast.147), channel_id=1, source_target_pairs={{0,8},{1,9},{2,10},{3,11},{4,12},{5,13},{6,14},{7,15},{8,0},{9,1},... | collective-permute-start | bytes 49160 | tf_op jit(solution)/shard_map/ppermute | solution.py:88
  232.3 8.0 %collective-permute-start.10 = (bf16[64,128]{1,0:T(8,128)(2,1)S(1)}, bf16[64,128]{1,0:T(8,128)(2,1)S(1)}, u32[]{:S(2)}, u32[]{:S(2)}) collective-permute-start(bf16[64,128]{1,0:T(8,128)(2,1)S(1)} %bitcast.146), channel_id=1, source_target_pairs={{0,9},{1,8},{2,11},{3,10},{4,13},{5,12},{6,15},{7,14},{8,1},{9,0},... | collective-permute-start | bytes 49160 | tf_op jit(solution)/shard_map/ppermute | solution.py:88
  233.0 9.9 %collective-permute-start.11 = (bf16[64,128]{1,0:T(8,128)(2,1)S(1)}, bf16[64,128]{1,0:T(8,128)(2,1)S(1)}, u32[]{:S(2)}, u32[]{:S(2)}) collective-permute-start(bf16[64,128]{1,0:T(8,128)(2,1)S(1)} %bitcast.145), channel_id=1, source_target_pairs={{0,10},{1,11},{2,8},{3,9},{4,14},{5,15},{6,12},{7,13},{8,2},{9,3},... | collective-permute-start | bytes 49160 | tf_op jit(solution)/shard_map/ppermute | solution.py:88
  236.0 8.6 %collective-permute-start.12 = (bf16[64,128]{1,0:T(8,128)(2,1)S(1)}, bf16[64,128]{1,0:T(8,128)(2,1)S(1)}, u32[]{:S(2)}, u32[]{:S(2)}) collective-permute-start(bf16[64,128]{1,0:T(8,128)(2,1)S(1)} %bitcast.144), channel_id=1, source_target_pairs={{0,11},{1,10},{2,9},{3,8},{4,15},{5,14},{6,13},{7,12},{8,3},{9,2},... | collective-permute-start | bytes 49160 | tf_op jit(solution)/shard_map/ppermute | solution.py:88
  236.5 8.0 %collective-permute-start.13 = (bf16[64,128]{1,0:T(8,128)(2,1)S(1)}, bf16[64,128]{1,0:T(8,128)(2,1)S(1)}, u32[]{:S(2)}, u32[]{:S(2)}) collective-permute-start(bf16[64,128]{1,0:T(8,128)(2,1)S(1)} %bitcast.143), channel_id=1, source_target_pairs={{0,12},{1,13},{2,14},{3,15},{4,8},{5,9},{6,10},{7,11},{8,4},{9,5},... | collective-permute-start | bytes 49160 | tf_op jit(solution)/shard_map/ppermute | solution.py:88
  239.1 5.5 %collective-permute-start.14 = (bf16[64,128]{1,0:T(8,128)(2,1)S(1)}, bf16[64,128]{1,0:T(8,128)(2,1)S(1)}, u32[]{:S(2)}, u32[]{:S(2)}) collective-permute-start(bf16[64,128]{1,0:T(8,128)(2,1)S(1)} %bitcast.142), channel_id=1, source_target_pairs={{0,13},{1,12},{2,15},{3,14},{4,9},{5,8},{6,11},{7,10},{8,5},{9,4},... | collective-permute-start | bytes 49160 | tf_op jit(solution)/shard_map/ppermute | solution.py:88
  240.3 5.4 %collective-permute-start.15 = (bf16[64,128]{1,0:T(8,128)(2,1)S(1)}, bf16[64,128]{1,0:T(8,128)(2,1)S(1)}, u32[]{:S(2)}, u32[]{:S(2)}) collective-permute-start(bf16[64,128]{1,0:T(8,128)(2,1)S(1)} %bitcast.141), channel_id=1, source_target_pairs={{0,14},{1,15},{2,12},{3,13},{4,10},{5,11},{6,8},{7,9},{8,6},{9,7},... | collective-permute-start | bytes 49160 | tf_op jit(solution)/shard_map/ppermute | solution.py:88
  242.9 6.3 %collective-permute-start.16 = (bf16[64,128]{1,0:T(8,128)(2,1)S(1)}, bf16[64,128]{1,0:T(8,128)(2,1)S(1)}, u32[]{:S(2)}, u32[]{:S(2)}) collective-permute-start(bf16[64,128]{1,0:T(8,128)(2,1)S(1)} %bitcast.140), channel_id=1, source_target_pairs={{0,15},{1,14},{2,13},{3,12},{4,11},{5,10},{6,9},{7,8},{8,7},{9,6},... | collective-permute-start | bytes 49160 | tf_op jit(solution)/shard_map/ppermute | solution.py:88
  244.6 12.2 %copy-start.3 = (s32[1,4]{1,0:T(1,128)S(1)}, s32[1,4]{1,0:T(1,128)}, u32[]{:S(2)}) copy-start(s32[1,4]{1,0:T(1,128)} %param.15) | copy-start | bytes 52
  250.0 104.8 %copy-start.2 = (s32[4]{0:T(128)S(1)}, s32[4]{0:T(128)}, u32[]{:S(2)}) copy-start(s32[4]{0:T(128)} %param.17) | copy-start | bytes 52
  250.6 9.5 %collective-permute-start.20 = (bf16[128,128]{1,0:T(8,128)(2,1)S(1)}, bf16[128,128]{1,0:T(8,128)(2,1)S(1)}, u32[]{:S(2)}, u32[]{:S(2)}) collective-permute-start(bf16[128,128]{1,0:T(8,128)(2,1)S(1)} %multiply_convert_fusion), channel_id=1, source_target_pairs={{4,0},{5,1},{6,2},{7,3},{8,4},{9,5},{10,6},{11,7},{12,8},{13,9},{1... | collective-permute-start | bytes 98312 | tf_op jit(solution)/shard_map/ppermute | solution.py:36
  251.9 8.5 %collective-permute-start.19 = (bf16[128,128]{1,0:T(8,128)(2,1)S(1)}, bf16[128,128]{1,0:T(8,128)(2,1)S(1)}, u32[]{:S(2)}, u32[]{:S(2)}) collective-permute-start(bf16[128,128]{1,0:T(8,128)(2,1)S(1)} %multiply_convert_fusion), channel_id=1, source_target_pairs={{3,0},{4,1},{5,2},{6,3},{7,4},{8,5},{9,6},{10,7},{11,8},{12,9},{13... | collective-permute-start | bytes 98312 | tf_op jit(solution)/shard_map/ppermute | solution.py:36
  253.2 7.2 %collective-permute-start.18 = (bf16[128,128]{1,0:T(8,128)(2,1)S(1)}, bf16[128,128]{1,0:T(8,128)(2,1)S(1)}, u32[]{:S(2)}, u32[]{:S(2)}) collective-permute-start(bf16[128,128]{1,0:T(8,128)(2,1)S(1)} %multiply_convert_fusion), channel_id=1, source_target_pairs={{2,0},{3,1},{4,2},{5,3},{6,4},{7,5},{8,6},{9,7},{10,8},{11,9},{12,... | collective-permute-start | bytes 98312 | tf_op jit(solution)/shard_map/ppermute | solution.py:36
  254.5 6.2 %collective-permute-start.17 = (bf16[128,128]{1,0:T(8,128)(2,1)S(1)}, bf16[128,128]{1,0:T(8,128)(2,1)S(1)}, u32[]{:S(2)}, u32[]{:S(2)}) collective-permute-start(bf16[128,128]{1,0:T(8,128)(2,1)S(1)} %multiply_convert_fusion), channel_id=1, source_target_pairs={{1,0},{2,1},{3,2},{4,3},{5,4},{6,5},{7,6},{8,7},{9,8},{10,9},{11,1... | collective-permute-start | bytes 98312 | tf_op jit(solution)/shard_map/ppermute | solution.py:36
Sparse Core Ops, SparseCore 0:
  261.5 93.3 all-reduce.1
